TPU v7x, 256 devices: a whole 4x4x8 slice. The times are simulated.
256 devices in a mesh: tok: 32 (over x, y, core), head: 8 (over z).
Axes of the slice: x: 4, y: 4, z: 8, core: 2. Of those that a mesh axis runs over, the one named last changes fastest.
Arguments:
- queries: bfloat16 [8192, 32, 128], P(('tok', 'head')), may hold values from -8 to 8
- keys: bfloat16 [8192, 8, 128], P(('tok', 'head')), may hold values from -8 to 8
- values: bfloat16 [8192, 8, 128], P(('tok', 'head')), may hold values from -6 to 6
- grad_out: bfloat16 [8192, 32, 128], P(('tok', 'head')), may hold values from -6 to 6
- ancestry: int32 [64, 16], replicated, may hold values from -1 to 63, as said below
Outputs:
- grad_queries: bfloat16 [8192, 32, 128], P(('tok', 'head'))
- grad_keys: bfloat16 [8192, 8, 128], P(('tok', 'head'))
- grad_values: bfloat16 [8192, 8, 128], P(('tok', 'head'))
Inputs may be any that keep to these rules, and one draw needn't show every extreme that they name: `ancestry`: row a lists the ancestor blocks of block a, nearest first, then -1 entries. Every ancestor is a block of the same tok index as a (same index // 2) or the first block of some tok index (an index that is a multiple of 2). Some block has exactly 16 ancestors.
All inputs are finite; a program needn't handle non-finite values.
Results may differ from a plain program's by a relative error of at most 0.0097.
Values may be sent and summed in bfloat16 or wider, within the bound.
A program may use at most 64 MiB of HBM per device.

v0:
```python
import math

import jax
import jax.numpy as jnp
from jax import lax
from jax.experimental import pallas as pl
from jax.experimental.pallas import tpu as pltpu
from jax.sharding import PartitionSpec as P

BLK = 128
HD = 128
GROUP = 4
HEADS = 8
NX, NY, NC = 4, 4, 2
NT = NX * NY * NC
SLICE = 32
DEPTH = 16
SLOTS = DEPTH + 1
ZERO_SLOT = SLOTS
POOL = NT + 1
ROWS = BLK * GROUP
KEYS = SLOTS * BLK
FACTOR = 1.0 / math.sqrt(HD)
SCALE2 = FACTOR * math.log2(math.e)
HIDDEN = -1e30
GS = 8
Z_ORDER = (4, 3, 5, 2, 6, 1, 7)
AROUND = sorted(((d, e) for d in range(NX) for e in range(NY) if d or e), key=lambda o: -sum(min(n, 4 - n) for n in o))
VMEM_LIMIT = 56 * 1024 * 1024
MESH = pl.DeviceIdType.MESH


def remote(src, dst, send_sem, recv_sem, **where):
    return pltpu.make_async_remote_copy(
        src_ref=src,
        dst_ref=dst,
        send_sem=send_sem,
        recv_sem=recv_sem,
        device_id=where,
        device_id_type=MESH,
    )


def tok_at(x, y, c):
    return (x % NX) * (NY * NC) + (y % NY) * NC + c


def one_hot(source):
    rows = lax.broadcasted_iota(jnp.int32, (256, 256), 0)
    cols = lax.broadcasted_iota(jnp.int32, (256, 256), 1)
    return jnp.where(source(rows) == cols, 1.0, 0.0).astype(jnp.bfloat16)


def exact_dot(picks, rows):
    return jnp.dot(picks, rows, preferred_element_type=jnp.float32).astype(jnp.bfloat16)


def regroup(i):
    return (i // 4 % 8) * 32 + (i // 32) * 4 + i % 4


def kv_heads_first(i):
    return (i % 32) * 8 + i // 32


def kv_tokens_first(i):
    return (i % 8) * 32 + i // 8


def fold(tile, op):
    return op(tile.reshape(-1, 8, ROWS), axis=0)


def f32_dot(a, b):
    return jnp.dot(a, b, preferred_element_type=jnp.float32)


def kernel(
    anc_hbm, q_hbm, k_hbm, v_hbm, g_hbm,
    gq_ref, gk_ref, gv_ref,
    anc, q_raw, k_raw, v_raw, g_raw, load_sem,
    ks, vs, qs, gs, q_in, g_in, kpool, vpool,
    chain, inverse, score0, score1, dprob0, dprob1, dscore0, dscore1, parts,
    dvpool, dkpool, core_in, plane, rs_in, home, home_in, dqs, dq_in,
    in_send, in_recv, pool_send, pool_recv, share_send, share_recv,
    half_send, half_recv, rs_send, rs_recv, home_send, home_recv, dq_send, dq_recv,
):
    t = lax.axis_index("tok")
    z = lax.axis_index("head")
    x, y, c = t // (NY * NC), (t // NC) % NY, t % NC
    sibling = tok_at(x, y, 1 - c)
    sent = []

    def launch(copy):
        copy.start()
        sent.append(copy)
        return copy

    def settle():
        while sent:
            sent.pop(0).wait_send()

    loads = []
    for i, (src, dst) in enumerate(((k_hbm, k_raw), (v_hbm, v_raw), (q_hbm, q_raw), (g_hbm, g_raw), (anc_hbm, anc))):
        load = pltpu.make_async_copy(src, dst, load_sem.at[i])
        load.start()
        loads.append(load)
    barrier = pltpu.get_barrier_semaphore()
    for dz in range(1, HEADS):
        pl.semaphore_signal(barrier, inc=1, device_id={"head": (z + dz) % HEADS}, device_id_type=MESH)
    for d, e in AROUND:
        pl.semaphore_signal(barrier, inc=1, device_id={"tok": tok_at(x + d, y + e, c)}, device_id_type=MESH)
    pl.semaphore_signal(barrier, inc=1, device_id={"tok": sibling}, device_id_type=MESH)

    slot = jnp.where(z < 4, t, NT)
    rows = pl.ds(pl.multiple_of((z % 4) * SLICE, SLICE), SLICE)
    arrivals = [[], [], [], []]

    def send_kv(i, src, pool):
        for dz in Z_ORDER:
            to = (z + dz) % HEADS
            copy = remote(src.at[to], pool.at[slot, rows, :], in_send.at[i, dz], in_recv.at[i, dz], head=to)
            arrivals[i].append(launch(copy))

    def send_heads(i, src, into):
        for dz in Z_ORDER:
            to = (z + dz) % HEADS
            copy = remote(src.at[to], into.at[z], in_send.at[i, dz], in_recv.at[i, dz], head=to)
            arrivals[i].append(launch(copy))

    def group_kv(i, raw, out, pool):
        loads[i].wait()
        out[...] = exact_dot(kv_picks, raw[...]).reshape(HEADS, SLICE, HD)
        pool[slot, rows, :] = out[z]

    def group_heads(i, raw, out, into):
        loads[i].wait()
        for o in range(4):
            moved = exact_dot(picks, raw[o * 256 : (o + 1) * 256, :])
            out[:, o * 32 : (o + 1) * 32, :] = moved.reshape(HEADS, 32, HD)
        into[z] = out[z]

    kv_picks = one_hot(kv_heads_first)
    group_kv(0, k_raw, ks, kpool)
    pl.semaphore_wait(barrier, HEADS - 1 + len(AROUND) + 1)
    send_kv(0, ks, kpool)
    group_kv(1, v_raw, vs, vpool)
    send_kv(1, vs, vpool)
    picks = one_hot(regroup)
    group_heads(2, q_raw, qs, q_in)
    send_heads(2, qs, q_in)
    group_heads(3, g_raw, gs, g_in)
    send_heads(3, gs, g_in)

    pools = (kpool, vpool)

    def pool_copy(i, d, e):
        ref = pools[i].at[t]
        return remote(ref, ref, pool_send.at[i, d, e], pool_recv.at[i, d, e], tok=tok_at(x + d, y + e, c))

    def share(i, d, e):
        ref = pools[i].at[tok_at(x - d, y - e, c)]
        return remote(ref, ref, share_send.at[i, d, e], share_recv.at[i, d, e], tok=sibling)

    def await_pool(i, d, e):
        ref = pools[i].at[tok_at(x - d, y - e, c)]
        remote(ref, ref, pool_send.at[i, d, e], pool_recv.at[i, d, e], tok=t).wait_recv()

    def await_share(i, d, e):
        ref = pools[i].at[tok_at(x - d, y - e, 1 - c)]
        remote(ref, ref, share_send.at[i, d, e], share_recv.at[i, d, e], tok=t).wait_recv()

    def forward(i, offsets):
        for d, e in offsets:
            await_pool(i, d, e)
            launch(share(i, d, e))

    for copy in arrivals[0]:
        copy.wait_recv()
    for d, e in AROUND:
        launch(pool_copy(0, d, e))
    launch(share(0, 0, 0))
    loads[4].wait()
    for b in range(2):
        chain[b, 0] = t if b == 0 else jnp.int32(NT)
        for s in range(DEPTH):
            a = anc[s, 2 * t + b]
            chain[b, 1 + s] = jnp.where(a < 0, -1, jnp.where(a % 2 == 1, NT, a // 2))

    @pl.loop(0, POOL)
    def _(p):
        for b in range(2):
            at = jnp.int32(ZERO_SLOT)
            for s in range(SLOTS):
                at = jnp.where(chain[b, s] == p, s, at)
            inverse[b, p] = at

    parts[:, ZERO_SLOT] = jnp.zeros((2, BLK, HD), jnp.float32)

    for copy in arrivals[1]:
        copy.wait_recv()
    forward(0, AROUND[:6])
    for d, e in AROUND:
        launch(pool_copy(1, d, e))
    launch(share(1, 0, 0))
    forward(0, AROUND[6:])
    for copy in arrivals[2]:
        copy.wait_recv()
    q = [q_in[4 * b : 4 * b + 4].reshape(ROWS, HD) for b in range(2)]
    qt = [tile.T for tile in q]
    for d, e in [(0, 0)] + AROUND:
        await_share(0, d, e)

    score, dprob, dscore = (score0, score1), (dprob0, dprob1), (dscore0, dscore1)

    def tiles(pool, b, first, count):
        found = [pool[jnp.maximum(chain[b, first + j], 0)] for j in range(count)]
        return found[0] if count == 1 else jnp.concatenate(found, axis=0)

    def rows_of(first, count):
        return pl.ds(first * BLK, count * BLK)

    def sweep(step, state):
        state = step(0, 1, state)
        return lax.fori_loop(0, DEPTH // GS, lambda n, state: step(1 + n * GS, GS, state), state)

    def beside(one, two):
        return lambda first, count, state: (one(first, count, state[0]), two(first, count, state[1]))

    def look(b):
        def step(first, count, top):
            s = f32_dot(tiles(kpool, b, first, count), qt[b])
            for j in range(count):
                part = s[j * BLK : (j + 1) * BLK]
                if count == 1:
                    key = lax.broadcasted_iota(jnp.int32, (BLK, ROWS), 0)
                    row = lax.broadcasted_iota(jnp.int32, (BLK, ROWS), 1)
                    part = jnp.where(key * GROUP <= row, part, HIDDEN)
                else:
                    part = part + jnp.where(chain[b, first + j] >= 0, 0.0, HIDDEN)
                score[b][rows_of(first + j, 1), :] = part
                top = jnp.maximum(top, fold(part, jnp.max))
            return top

        return step

    def top_of(top):
        return jnp.max(top, axis=0, keepdims=True) * SCALE2

    def soften(b, top):
        def step(first, count, total):
            e = jnp.exp2(score[b][rows_of(first, count), :] * SCALE2 - top)
            score[b][rows_of(first, count), :] = e
            return total + fold(e, jnp.sum)

        return step

    def over_of(total):
        return 1.0 / jnp.sum(total, axis=0, keepdims=True)

    def value_part(b, over):
        def step(first, count, state):
            p = score[b][rows_of(first, count), :] * over
            dv = f32_dot(p.astype(jnp.bfloat16), g[b])
            for j in range(count):
                parts[b, first + j] = dv[j * BLK : (j + 1) * BLK]
            return state

        return step

    def cross(b):
        def step(first, count, weighted):
            dp = f32_dot(tiles(vpool, b, first, count), gt[b])
            dprob[b][rows_of(first, count), :] = dp
            return weighted + fold(score[b][rows_of(first, count), :] * dp, jnp.sum)

        return step

    def key_part(b, over, delta):
        def step(first, count, state):
            p = score[b][rows_of(first, count), :] * over
            ds = (p * (dprob[b][rows_of(first, count), :] - delta)).astype(jnp.bfloat16)
            dscore[b][rows_of(first, count), :] = ds
            dk = f32_dot(ds, q[b]) * FACTOR
            for j in range(count):
                parts[b, first + j] = dk[j * BLK : (j + 1) * BLK]
            return state

        return step

    def query_part(b):
        def step(first, count, dqt):
            return dqt + lax.dot_general(
                tiles(kpool, b, first, count), dscore[b][rows_of(first, count), :],
                (((0,), (0,)), ((), ())), preferred_element_type=jnp.float32,
            )

        return step

    halves = (dkpool, dvpool)

    def total_of(p):
        return parts[0, inverse[0, p]] + parts[1, inverse[1, p]]

    def half_copy(i, d, e):
        return remote(
            halves[i].at[d * NY + e], core_in.at[i, d, e], half_send.at[i, d, e], half_recv.at[i, d, e], tok=sibling
        )

    def rs_copy(i, d, e):
        return remote(
            plane.at[i, d, e], rs_in.at[i, d, e], rs_send.at[i, d, e], rs_recv.at[i, d, e], tok=tok_at(x + d, y + e, c)
        )

    def give_halves(i):
        for d, e in AROUND + [(0, 0)]:
            halves[i][d * NY + e] = total_of(tok_at(x + d, y + e, 1 - c)).astype(jnp.bfloat16)
            launch(half_copy(i, d, e))

    def give_homes(i):
        for d, e in AROUND:
            mine = total_of(tok_at(x + d, y + e, c))
            half_copy(i, d, e).wait_recv()
            plane[i, d, e] = (mine + core_in[i, d, e].astype(jnp.float32)).astype(jnp.bfloat16)
            launch(rs_copy(i, d, e))
        mine = total_of(t)
        half_copy(i, 0, 0).wait_recv()
        home[i, 4:8] = total_of(NT).astype(jnp.bfloat16).reshape(4, SLICE, HD)
        return mine + core_in[i, 0, 0].astype(jnp.float32)

    def to_tokens(i, total):
        for d, e in AROUND:
            rs_copy(i, d, e).wait_recv()
            total = total + rs_in[i, d, e].astype(jnp.float32)
        home[i, 0:4] = total.astype(jnp.bfloat16).reshape(4, SLICE, HD)
        copies = []
        for dz in Z_ORDER:
            to = (z + dz) % HEADS
            copies.append(launch(remote(home.at[i, to], home_in.at[i, z], home_send.at[i, dz], home_recv.at[i, dz], head=to)))
        home_in[i, z] = home[i, z]
        return copies

    start = jnp.full((8, ROWS), HIDDEN, jnp.float32)
    zero = jnp.zeros((8, ROWS), jnp.float32)
    none = jnp.int32(0)
    top0 = top_of(sweep(look(0), start))
    total0, top1 = sweep(beside(soften(0, top0), look(1)), (zero, start))
    over0, top1 = over_of(total0), top_of(top1)
    total1 = sweep(soften(1, top1), zero)
    over1 = over_of(total1)
    for copy in arrivals[3]:
        copy.wait_recv()
    g = [g_in[4 * b : 4 * b + 4].reshape(ROWS, HD) for b in range(2)]
    gt = [tile.T for tile in g]
    sweep(beside(value_part(0, over0), value_part(1, over1)), (none, none))
    give_halves(1)
    forward(1, AROUND)
    mine_v = give_homes(1)
    for d, e in [(0, 0)] + AROUND:
        await_share(1, d, e)
    weighted0 = sweep(cross(0), zero)
    delta0 = jnp.sum(weighted0, axis=0, keepdims=True) * over0
    _, weighted1 = sweep(beside(key_part(0, over0, delta0), cross(1)), (none, zero))
    delta1 = jnp.sum(weighted1, axis=0, keepdims=True) * over1
    sweep(key_part(1, over1, delta1), none)
    give_halves(0)

    empty = jnp.zeros((HD, ROWS), jnp.float32)
    dqt = sweep(beside(query_part(0), query_part(1)), (empty, empty))
    for b in range(2):
        dqs[4 * b : 4 * b + 4] = (dqt[b] * FACTOR).T.astype(jnp.bfloat16).reshape(4, SLICE * GROUP, HD)
    mine_k = give_homes(0)
    dq_copies = []
    for dz in Z_ORDER:
        to = (z + dz) % HEADS
        dq_copies.append(launch(remote(dqs.at[to], dq_in.at[z], dq_send.at[dz], dq_recv.at[dz], head=to)))
    dq_in[z] = dqs[z]
    v_copies = to_tokens(1, mine_v)
    settle()
    k_copies = to_tokens(0, mine_k)

    picks = one_hot(regroup)
    for copy in dq_copies:
        copy.wait_recv()
    for o in range(4):
        moved = dq_in[:, o * 32 : (o + 1) * 32, :].reshape(256, HD)
        gq_ref[o * 256 : (o + 1) * 256, :] = exact_dot(picks, moved)
    picks = one_hot(kv_tokens_first)
    for copy in v_copies:
        copy.wait_recv()
    gv_ref[...] = exact_dot(picks, home_in[1].reshape(256, HD))
    for copy in k_copies:
        copy.wait_recv()
    gk_ref[...] = exact_dot(picks, home_in[0].reshape(256, HD))
    settle()


def store_kernel(gq, gk, gv, gq_out, gk_out, gv_out, sem):
    copies = [
        pltpu.make_async_copy(src, dst, sem.at[i])
        for i, (src, dst) in enumerate(((gq, gq_out), (gk, gk_out), (gv, gv_out)))
    ]
    for copy in copies:
        copy.start()
    for copy in copies:
        copy.wait()


def whole():
    return pl.BlockSpec(memory_space=pltpu.VMEM)


def anywhere():
    return pl.BlockSpec(memory_space=pl.ANY)


def shape(*dims):
    return jax.ShapeDtypeStruct(dims, jnp.bfloat16)


def buffer(*dims, dtype=jnp.bfloat16):
    return pltpu.VMEM(dims, dtype)


def sems(*dims):
    return pltpu.SemaphoreType.DMA(dims)


def local(queries, keys, values, grad_out, ancestry):
    rows = SLICE * GROUP
    results = (shape(SLICE * 32, HD), shape(SLICE * HEADS, HD), shape(SLICE * HEADS, HD))
    grads = pl.pallas_call(
        kernel,
        out_shape=tuple(pltpu.VMEM(r.shape, r.dtype) for r in results),
        in_specs=[anywhere()] * 5,
        out_specs=(whole(),) * 3,
        scratch_shapes=[
            pltpu.SMEM((DEPTH, 2 * NT), jnp.int32),
            buffer(SLICE * 32, HD), buffer(SLICE * HEADS, HD), buffer(SLICE * HEADS, HD), buffer(SLICE * 32, HD),
            sems(5),
            buffer(HEADS, SLICE, HD), buffer(HEADS, SLICE, HD), buffer(HEADS, rows, HD), buffer(HEADS, rows, HD),
            buffer(HEADS, rows, HD), buffer(HEADS, rows, HD), buffer(POOL, BLK, HD), buffer(POOL, BLK, HD),
            pltpu.SMEM((2, SLOTS), jnp.int32), pltpu.SMEM((2, POOL), jnp.int32),
            buffer(KEYS, ROWS, dtype=jnp.float32), buffer(KEYS, ROWS, dtype=jnp.float32),
            buffer(KEYS, ROWS, dtype=jnp.float32), buffer(KEYS, ROWS, dtype=jnp.float32),
            buffer(KEYS, ROWS), buffer(KEYS, ROWS),
            buffer(2, SLOTS + 1, BLK, HD, dtype=jnp.float32),
            buffer(NX * NY, BLK, HD), buffer(NX * NY, BLK, HD),
            buffer(2, NX, NY, BLK, HD), buffer(2, NX, NY, BLK, HD), buffer(2, NX, NY, BLK, HD),
            buffer(2, HEADS, SLICE, HD), buffer(2, HEADS, SLICE, HD), buffer(HEADS, rows, HD), buffer(HEADS, rows, HD),
            sems(4, 8), sems(4, 8), sems(2, 4, 4), sems(2, 4, 4), sems(2, 4, 4), sems(2, 4, 4),
            sems(2, 4, 4), sems(2, 4, 4), sems(2, 4, 4), sems(2, 4, 4), sems(2, 8), sems(2, 8), sems(8), sems(8),
        ],
        compiler_params=pltpu.CompilerParams(collective_id=0, has_side_effects=True, vmem_limit_bytes=VMEM_LIMIT),
        name="backward",
    )(
        ancestry.T,
        queries.reshape(SLICE * 32, HD),
        keys.reshape(SLICE * HEADS, HD),
        values.reshape(SLICE * HEADS, HD),
        grad_out.reshape(SLICE * 32, HD),
    )
    gq, gk, gv = pl.pallas_call(
        store_kernel,
        out_shape=results,
        in_specs=[whole()] * 3,
        out_specs=(anywhere(),) * 3,
        scratch_shapes=[sems(3)],
        name="store",
    )(*(pltpu.with_memory_space_constraint(r, pltpu.VMEM) for r in grads))
    return (
        gq.reshape(SLICE, 32, HD),
        gk.reshape(SLICE, HEADS, HD),
        gv.reshape(SLICE, HEADS, HD),
    )


def solution(mesh):
    placed = P(("tok", "head"), None, None)
    return jax.shard_map(
        local,
        mesh=mesh,
        in_specs=(placed, placed, placed, placed, P()),
        out_specs=(placed, placed, placed),
        check_vma=False,
    )
```

profile of v0, /device:TPU:1, one launch (start us, length us, event | category | flops | bytes accessed | tf_op | source)
XLA Modules:
  0.0 54.8 jit_solution(13258034617185759826)
XLA Ops:
  0.6 53.4 %backward.1 = (bf16[1024,128]{1,0:T(8,128)(2,1)S(1)}, bf16[256,128]{1,0:T(8,128)(2,1)S(1)}, bf16[256,128]{1,0:T(8,128)(2,1)S(1)}) custom-call(s32[16,64]{1,0:T(8,128)} %bitcast.12, bf16[1024,128]{1,0:T(8,128)(2,1)} %bitcast.8, bf16[256,128]{1,0:T(8,128)(2,1)} %bitcast.10, bf16[256,128]{1,0:T(8,128)(2,1)} %bitcast.11, bf16[1024,128]{1,0:T(8,128)(2,1)} %bitcast.9), custom_call_target="tpu_custom_call" | custom-call | tf_op jit(solution)/shard_map/backward/pallas_call | solution.py:432
  54.1 0.8 %store.1 = (bf16[1024,128]{1,0:T(8,128)(2,1)}, bf16[256,128]{1,0:T(8,128)(2,1)}, bf16[256,128]{1,0:T(8,128)(2,1)}) custom-call(bf16[1024,128]{1,0:T(8,128)(2,1)S(1)} %get-tuple-element.9.gq, bf16[256,128]{1,0:T(8,128)(2,1)S(1)} %get-tuple-element.10.gk, bf16[256,128]{1,0:T(8,128)(2,1)S(1)} %get-tuple-element.11.gv), custom_call_target="tpu_custom_call" | custom-call | tf_op jit(solution)/shard_map/store/pallas_call | solution.py:463
where the time goes:
time: 54.9 us; the launch traced here: 54.8 us
  Pallas kernels  54.2 us (99%)
  between operations  0.64 us (1%)
    pallas_call x1, Pallas kernels, local(): pl.pallas_call(kernel, out_shape=tuple((pltpu.VMEM(r.shape, r.dtype) for...  53.4 us

commit v1 on v0

--- a/solution.py
+++ b/solution.py
@@ -144,11 +144,11 @@
     group_kv(0, k_raw, ks, kpool)
     pl.semaphore_wait(barrier, HEADS - 1 + len(AROUND) + 1)
     send_kv(0, ks, kpool)
-    group_kv(1, v_raw, vs, vpool)
-    send_kv(1, vs, vpool)
     picks = one_hot(regroup)
     group_heads(2, q_raw, qs, q_in)
     send_heads(2, qs, q_in)
+    group_kv(1, v_raw, vs, vpool)
+    send_kv(1, vs, vpool)
     group_heads(3, g_raw, gs, g_in)
     send_heads(3, gs, g_in)
 
@@ -199,11 +199,11 @@
 
     for copy in arrivals[1]:
         copy.wait_recv()
-    forward(0, AROUND[:6])
+    forward(0, AROUND[:15])
     for d, e in AROUND:
         launch(pool_copy(1, d, e))
     launch(share(1, 0, 0))
-    forward(0, AROUND[6:])
+    forward(0, AROUND[15:])
     for copy in arrivals[2]:
         copy.wait_recv()
     q = [q_in[4 * b : 4 * b + 4].reshape(ROWS, HD) for b in range(2)]
@@ -343,26 +343,23 @@
     start = jnp.full((8, ROWS), HIDDEN, jnp.float32)
     zero = jnp.zeros((8, ROWS), jnp.float32)
     none = jnp.int32(0)
-    top0 = top_of(sweep(look(0), start))
-    total0, top1 = sweep(beside(soften(0, top0), look(1)), (zero, start))
-    over0, top1 = over_of(total0), top_of(top1)
-    total1 = sweep(soften(1, top1), zero)
-    over1 = over_of(total1)
+    top0, top1 = sweep(beside(look(0), look(1)), (start, start))
+    total0, total1 = sweep(beside(soften(0, top_of(top0)), soften(1, top_of(top1))), (zero, zero))
+    over0, over1 = over_of(total0), over_of(total1)
     for copy in arrivals[3]:
         copy.wait_recv()
     g = [g_in[4 * b : 4 * b + 4].reshape(ROWS, HD) for b in range(2)]
-    gt = [tile.T for tile in g]
     sweep(beside(value_part(0, over0), value_part(1, over1)), (none, none))
     give_halves(1)
+    gt = [tile.T for tile in g]
     forward(1, AROUND)
     mine_v = give_homes(1)
     for d, e in [(0, 0)] + AROUND:
         await_share(1, d, e)
-    weighted0 = sweep(cross(0), zero)
-    delta0 = jnp.sum(weighted0, axis=0, keepdims=True) * over0
-    _, weighted1 = sweep(beside(key_part(0, over0, delta0), cross(1)), (none, zero))
-    delta1 = jnp.sum(weighted1, axis=0, keepdims=True) * over1
-    sweep(key_part(1, over1, delta1), none)
+    weighted = sweep(beside(cross(0), cross(1)), (zero, zero))
+    delta0 = jnp.sum(weighted[0], axis=0, keepdims=True) * over0
+    delta1 = jnp.sum(weighted[1], axis=0, keepdims=True) * over1
+    sweep(beside(key_part(0, over0, delta0), key_part(1, over1, delta1)), (none, none))
     give_halves(0)
 
     empty = jnp.zeros((HD, ROWS), jnp.float32)

time: 54.9 us -> 53.6 us (0.976)
  Pallas kernels: 54.2 us -> 52.9 us
    pallas_call x1, Pallas kernels: 53.4 us -> 52.1 us  [local(): pl.pallas_call(kernel, out_shape=tuple((pltpu.VMEM(r.shape, r.dtype) for...]
where the time goes in v1:
time: 53.6 us; the launch traced here: 53.5 us
  Pallas kernels  52.9 us (99%)
  between operations  0.64 us (1%)
    pallas_call x1, Pallas kernels, local(): pl.pallas_call(kernel, out_shape=tuple((pltpu.VMEM(r.shape, r.dtype) for...  52.1 us

profile of v1, /device:TPU:1, one launch (start us, length us, event | category | flops | bytes accessed | tf_op | source)
XLA Modules:
  0.0 53.5 jit_solution(11416882984614813370)
XLA Ops:
  0.6 52.1 %backward.1 = (bf16[1024,128]{1,0:T(8,128)(2,1)S(1)}, bf16[256,128]{1,0:T(8,128)(2,1)S(1)}, bf16[256,128]{1,0:T(8,128)(2,1)S(1)}) custom-call(s32[16,64]{1,0:T(8,128)} %bitcast.12, bf16[1024,128]{1,0:T(8,128)(2,1)} %bitcast.8, bf16[256,128]{1,0:T(8,128)(2,1)} %bitcast.10, bf16[256,128]{1,0:T(8,128)(2,1)} %bitcast.11, bf16[1024,128]{1,0:T(8,128)(2,1)} %bitcast.9), custom_call_target="tpu_custom_call" | custom-call | tf_op jit(solution)/shard_map/backward/pallas_call | solution.py:429
  52.7 0.8 %store.1 = (bf16[1024,128]{1,0:T(8,128)(2,1)}, bf16[256,128]{1,0:T(8,128)(2,1)}, bf16[256,128]{1,0:T(8,128)(2,1)}) custom-call(bf16[1024,128]{1,0:T(8,128)(2,1)S(1)} %get-tuple-element.9.gq, bf16[256,128]{1,0:T(8,128)(2,1)S(1)} %get-tuple-element.10.gk, bf16[256,128]{1,0:T(8,128)(2,1)S(1)} %get-tuple-element.11.gv), custom_call_target="tpu_custom_call" | custom-call | tf_op jit(solution)/shard_map/store/pallas_call | solution.py:460

commit v2 on v1

--- a/solution.py
+++ b/solution.py
@@ -26,6 +26,7 @@
 GS = 8
 Z_ORDER = (4, 3, 5, 2, 6, 1, 7)
 AROUND = sorted(((d, e) for d in range(NX) for e in range(NY) if d or e), key=lambda o: -sum(min(n, 4 - n) for n in o))
+NEAR = AROUND[::-1]
 VMEM_LIMIT = 56 * 1024 * 1024
 MESH = pl.DeviceIdType.MESH
 
@@ -100,17 +101,17 @@
         while sent:
             sent.pop(0).wait_send()
 
+    barrier = pltpu.get_barrier_semaphore()
+    for dz in Z_ORDER:
+        pl.semaphore_signal(barrier, inc=1, device_id={"head": (z + dz) % HEADS}, device_id_type=MESH)
+    for d, e in AROUND:
+        pl.semaphore_signal(barrier, inc=1, device_id={"tok": tok_at(x + d, y + e, c)}, device_id_type=MESH)
+    pl.semaphore_signal(barrier, inc=1, device_id={"tok": sibling}, device_id_type=MESH)
     loads = []
     for i, (src, dst) in enumerate(((k_hbm, k_raw), (v_hbm, v_raw), (q_hbm, q_raw), (g_hbm, g_raw), (anc_hbm, anc))):
         load = pltpu.make_async_copy(src, dst, load_sem.at[i])
         load.start()
         loads.append(load)
-    barrier = pltpu.get_barrier_semaphore()
-    for dz in range(1, HEADS):
-        pl.semaphore_signal(barrier, inc=1, device_id={"head": (z + dz) % HEADS}, device_id_type=MESH)
-    for d, e in AROUND:
-        pl.semaphore_signal(barrier, inc=1, device_id={"tok": tok_at(x + d, y + e, c)}, device_id_type=MESH)
-    pl.semaphore_signal(barrier, inc=1, device_id={"tok": sibling}, device_id_type=MESH)
 
     slot = jnp.where(z < 4, t, NT)
     rows = pl.ds(pl.multiple_of((z % 4) * SLICE, SLICE), SLICE)
@@ -199,11 +200,10 @@
 
     for copy in arrivals[1]:
         copy.wait_recv()
-    forward(0, AROUND[:15])
     for d, e in AROUND:
         launch(pool_copy(1, d, e))
     launch(share(1, 0, 0))
-    forward(0, AROUND[15:])
+    forward(0, NEAR)
     for copy in arrivals[2]:
         copy.wait_recv()
     q = [q_in[4 * b : 4 * b + 4].reshape(ROWS, HD) for b in range(2)]
@@ -329,7 +329,7 @@
         return mine + core_in[i, 0, 0].astype(jnp.float32)
 
     def to_tokens(i, total):
-        for d, e in AROUND:
+        for d, e in NEAR:
             rs_copy(i, d, e).wait_recv()
             total = total + rs_in[i, d, e].astype(jnp.float32)
         home[i, 0:4] = total.astype(jnp.bfloat16).reshape(4, SLICE, HD)
@@ -352,7 +352,7 @@
     sweep(beside(value_part(0, over0), value_part(1, over1)), (none, none))
     give_halves(1)
     gt = [tile.T for tile in g]
-    forward(1, AROUND)
+    forward(1, NEAR)
     mine_v = give_homes(1)
     for d, e in [(0, 0)] + AROUND:
         await_share(1, d, e)

time: 53.6 us -> 53.1 us (level)
  Pallas kernels: 52.9 us -> 52.3 us
where the time goes in v2:
time: 53.1 us; the launch traced here: 53 us
  Pallas kernels  52.3 us (98%)
  between operations  0.64 us (1%)
    pallas_call x1, Pallas kernels, local(): pl.pallas_call(kernel, out_shape=tuple((pltpu.VMEM(r.shape, r.dtype) for...  51.6 us

profile of v2, /device:TPU:1, one launch (start us, length us, event | category | flops | bytes accessed | tf_op | source)
XLA Modules:
  0.0 53.0 jit_solution(10108423448362864288)
XLA Ops:
  0.6 51.6 %backward.1 = (bf16[1024,128]{1,0:T(8,128)(2,1)S(1)}, bf16[256,128]{1,0:T(8,128)(2,1)S(1)}, bf16[256,128]{1,0:T(8,128)(2,1)S(1)}) custom-call(s32[16,64]{1,0:T(8,128)} %bitcast.12, bf16[1024,128]{1,0:T(8,128)(2,1)} %bitcast.8, bf16[256,128]{1,0:T(8,128)(2,1)} %bitcast.10, bf16[256,128]{1,0:T(8,128)(2,1)} %bitcast.11, bf16[1024,128]{1,0:T(8,128)(2,1)} %bitcast.9), custom_call_target="tpu_custom_call" | custom-call | tf_op jit(solution)/shard_map/backward/pallas_call | solution.py:429
  52.2 0.8 %store.1 = (bf16[1024,128]{1,0:T(8,128)(2,1)}, bf16[256,128]{1,0:T(8,128)(2,1)}, bf16[256,128]{1,0:T(8,128)(2,1)}) custom-call(bf16[1024,128]{1,0:T(8,128)(2,1)S(1)} %get-tuple-element.9.gq, bf16[256,128]{1,0:T(8,128)(2,1)S(1)} %get-tuple-element.10.gk, bf16[256,128]{1,0:T(8,128)(2,1)S(1)} %get-tuple-element.11.gv), custom_call_target="tpu_custom_call" | custom-call | tf_op jit(solution)/shard_map/store/pallas_call | solution.py:460
